TPU v7x, 32 devices: a whole 2x2x4 slice. The times are simulated.
32 devices in a mesh: row: 4 (over y, core), col: 2 (over x), rep: 4 (over z).
Axes of the slice: x: 2, y: 2, z: 4, core: 2. Of those that a mesh axis runs over, the one named last changes fastest.
Arguments:
- features: float32 [256, 4096], P('rep', ('col', 'row')), may hold values from -6 to 6
- weight: float32 [256, 256], replicated, may hold values from -0.375 to 0.375
- cotangent: float32 [256, 4096], P('rep', ('row', 'col')), may hold values from -6 to 6
- tile_values: float32 [1280, 128, 128], P(('row', 'col')), may hold values from -0.078125 to 0.078125
- tile_row: int32 [1280], P(('row', 'col')), may hold values from 0 to 7
- tile_col: int32 [1280], P(('row', 'col')), may hold values from 0 to 15
- tile_kind: int32 [1280], P(('row', 'col')), may hold values from 0 to 159
- tile_count: int32 [8], P(('row', 'col')), may hold values from 40 to 160, as said below
Outputs:
- output: float32 [256, 4096], P('rep', ('row', 'col'))
- input_grad: float32 [256, 4096], P('rep', ('col', 'row'))
- weight_grad: float32 [256, 256], P('rep')
Inputs may be any that keep to these rules, and one draw needn't show every extreme that they name: `tile_count`: a block's slots at or after its count are not part of the adjacency; some block uses all 160 slots. `tile_row`: slots may repeat a tile position; their tiles add. `tile_kind`: an index into the 160 stored tiles of the same block.
All inputs are finite; a program needn't handle non-finite values.
Results may differ from a plain program's by a relative error of at most 0.0001.
Values sent between devices are 32-bit elements; how exact they have to be, the bound alone decides.
A program may use at most 128 MiB of HBM per device.

v0:
```python
import functools

import jax
import jax.numpy as jnp
from jax import lax
from jax.experimental import pallas as pl
from jax.experimental.pallas import tpu as pltpu
from jax.sharding import PartitionSpec as P

MESH = pl.DeviceIdType.MESH
F32, BF16 = jnp.float32, jnp.bfloat16
DENSE_BYTES = 16 * 2**20
NT = (((1,), (1,)), ((), ()))
NN = (((1,), (0,)), ((), ()))


def split(x):
    high = x.astype(BF16)
    return high, (x - high.astype(F32)).astype(BF16)


def dot_split(stacked, high, b_high, b_low, dims):
    rows = high.shape[0]
    both = lax.dot_general(stacked, b_high, dims, preferred_element_type=F32)
    cross = lax.dot_general(high, b_low, dims, preferred_element_type=F32)
    return both[:rows] + both[rows:] + cross


def product(a, b, dims):
    a_high, a_low = split(a)
    return dot_split(jnp.concatenate([a_high, a_low], 0), a_high, *split(b), dims)


def chain_links(row_tiles, col_tiles, count, tile_row, tile_col):
    slots = tile_row.shape[1]
    queries = slots + row_tiles * col_tiles
    place = tile_row * col_tiles + tile_col
    shape = (slots, slots)
    key, query = (lax.broadcasted_iota(jnp.int32, shape, axis) for axis in (0, 1))
    keys = jnp.max(jnp.where(key == query, place, 0), axis=1, keepdims=True)

    def latest(hit, key):
        last = jnp.max(jnp.where(hit & (key < count), key, -1), axis=0, keepdims=True)
        return jnp.where(last < 0, slots, last)

    before = latest((keys == place) & (key < query), key)
    shape = (slots, row_tiles * col_tiles)
    key, query = (lax.broadcasted_iota(jnp.int32, shape, axis) for axis in (0, 1))
    return before, latest(keys == query, key)


def layer_kernel(
    n_row, n_col, n_rep, kind, count, tile_row, tile_col, features_in, weight_in, cotangent_in, values_in,
    output, input_grad, weight_grad,
    before_v, last_v, before, last, held, chain, weight, a_high, a_low, xs, xg, cg, yg, part, part_in, pre, hg, z_own, z_sib, z_far, w_own, w_in, w_all,
    l_sem, i_sem, t_sem, x_send, x_recv, c_send, c_recv, y_send, y_recv, p_send, p_recv, h_send, h_recv,
    s_send, s_recv, f_send, f_recv, w_send, w_recv, v_send, v_recv,
):
    row, col, rep = lax.axis_index("row"), lax.axis_index("col"), lax.axis_index("rep")
    n_y = n_row // 2
    core, y = lax.rem(row, 2), lax.div(row, 2)
    sibling = y * 2 + (1 - core)
    quarter, stretch = features_in.shape
    slots, edge, _ = held.shape
    tiles = stretch // edge
    peers = n_row * n_col
    me = row * n_col + col

    def peer(k):
        other = lax.rem(me + k, peers)
        return other, {"row": lax.div(other, n_col), "col": lax.rem(other, n_col)}

    def far(k):
        return lax.rem(y + k, n_y)

    def send(src, dst, send_sem, recv_sem, device):
        return pltpu.make_async_remote_copy(
            src_ref=src, dst_ref=dst, send_sem=send_sem, recv_sem=recv_sem,
            device_id=device, device_id_type=MESH,
        )

    barrier = pltpu.get_barrier_semaphore()
    for k in range(1, peers):
        pl.semaphore_signal(barrier, inc=1, device_id=peer(k)[1], device_id_type=MESH)

    @pl.when(rep > 0)
    def _():
        pl.semaphore_signal(barrier, inc=1, device_id={"rep": rep - 1}, device_id_type=MESH)

    @pl.when(rep < n_rep - 1)
    def _():
        pl.semaphore_signal(barrier, inc=1, device_id={"rep": rep + 1}, device_id_type=MESH)

    inputs = [
        pltpu.make_async_copy(features_in, xg.at[row], i_sem.at[0]),
        pltpu.make_async_copy(cotangent_in, cg.at[rep, 0], i_sem.at[1]),
        pltpu.make_async_copy(weight_in, weight, i_sem.at[2]),
    ]
    parts = t_sem.shape[0]
    size = slots // parts
    for k in range(parts):
        piece = pl.ds(k * size, size)
        inputs.append(pltpu.make_async_copy(values_in.at[piece], held.at[piece], t_sem.at[k]))
    for copy in inputs:
        copy.start()

    ends = jnp.where(rep == 0, 1, 0) + jnp.where(rep == n_rep - 1, 1, 0)
    pl.semaphore_wait(barrier, peers + 1 - ends)

    sent = []

    def start(*args):
        copy = send(*args)
        copy.start()
        sent.append(copy)

    def line_send(buf, send_sem, recv_sem, piece, gap, side, begin):
        origin = rep - gap * side
        go = (origin >= 0) & (origin < n_rep) & (rep + side >= 0) & (rep + side < n_rep)

        @pl.when(go)
        def _():
            copy = send(
                buf.at[origin, piece], buf.at[origin, piece],
                send_sem.at[(side + 1) // 2, gap, piece], recv_sem.at[origin, piece],
                {"rep": rep + side},
            )
            if begin:
                copy.start()
            else:
                copy.wait_send()

    def line_step(buf, send_sem, recv_sem, piece, gap):
        for side in (1, -1):
            if gap:
                origin = rep - gap * side

                @pl.when((origin >= 0) & (origin < n_rep))
                def _():
                    send(
                        buf.at[origin, piece], buf.at[origin, piece], send_sem.at[0, 0, 0],
                        recv_sem.at[origin, piece], {"rep": rep - side},
                    ).wait_recv()

            if gap < n_rep - 1:
                line_send(buf, send_sem, recv_sem, piece, gap, side, True)

    def arrived(buf, recv_sem, device):
        send(buf, buf, x_send.at[0], recv_sem, device).wait_recv()

    inputs[0].wait()
    for k in range(1, n_y):
        start(xg.at[row], xg.at[row], x_send.at[k], x_recv.at[row], {"row": far(k) * 2 + core})
    start(xg.at[row], xg.at[row], x_send.at[0], x_recv.at[row], {"row": sibling})
    inputs[1].wait()
    line_step(cg, c_send, c_recv, 0, 0)

    links = chain_links(
        n_col * tiles, n_row * tiles, count[0],
        tile_row[...].reshape(1, slots), tile_col[...].reshape(1, slots),
    )
    before_v[...], last_v[...] = links
    moves = [
        pltpu.make_async_copy(before_v, before, l_sem.at[0]),
        pltpu.make_async_copy(last_v, last, l_sem.at[1]),
    ]
    for copy in moves:
        copy.start()

    for copy in inputs[2:] + moves:
        copy.wait()
    chain[slots] = jnp.zeros((edge, edge), F32)

    @pl.loop(0, slots, unroll=4 if slots % 4 == 0 else 1)
    def _(slot):
        chain[slot] = held[kind[slot]] + chain[before[0, slot]]

    def ready(origin):
        high, low = split(xg[origin])
        both = jnp.concatenate([high.astype(F32), low.astype(F32)], 0).T
        xs[pl.ds(pl.multiple_of(origin * stretch, stretch), stretch), :] = both.astype(BF16)

    ready(row)
    for k in range(1, n_y):
        origin = far(k) * 2 + core
        arrived(xg.at[origin], x_recv.at[origin], {"row": origin})
        start(
            xg.at[origin], xg.at[origin], x_send.at[n_y + k - 1], x_recv.at[origin],
            {"row": sibling},
        )
        ready(origin)
    arrived(xg.at[sibling], x_recv.at[sibling], {"row": sibling})
    ready(sibling)
    line_step(cg, c_send, c_recv, 0, 1)

    pieces = yg.shape[1]
    short = stretch // pieces
    spans = [pl.ds(piece * short, short) for piece in range(pieces)]

    def dense(dest, piece):
        @pl.loop(0, short // edge)
        def _(i):
            first = (dest * tiles + piece * (short // edge) + i) * (n_row * tiles)
            rows = pl.ds(pl.multiple_of(piece * short + i * edge, edge), edge)
            for j in range(n_row * tiles):
                high, low = split(chain[last[0, first + j]])
                a_high[dest, rows, pl.ds(j * edge, edge)] = high
                a_low[dest, rows, pl.ds(j * edge, edge)] = low

    def aggregate_piece(dest, piece):
        nodes = xs[...]
        term = jnp.dot(a_high[dest, spans[piece], :], nodes, preferred_element_type=F32)
        term += jnp.dot(a_low[dest, spans[piece], :], nodes, preferred_element_type=F32)
        term = term.T
        return term[:quarter] + term[quarter:]

    def others(piece):
        for k in range(1, n_col):
            dest = lax.rem(col + k, n_col)
            dense(dest, piece)
            if k == 1 and piece == 0:
                for far_y in range(1, n_y):
                    origin = far(far_y) * 2 + (1 - core)
                    arrived(xg.at[origin], x_recv.at[origin], {"row": sibling})
                    ready(origin)
            part[dest, piece] = aggregate_piece(dest, piece)
            start(
                part.at[dest, piece], part_in.at[col, piece], p_send.at[k, piece],
                p_recv.at[col, piece], {"col": dest},
            )

    def own_part(piece):
        dense(col, piece)
        summed = aggregate_piece(col, piece)
        for k in range(1, n_col):
            other = lax.rem(col + k, n_col)
            arrived(part_in.at[other, piece], p_recv.at[other, piece], {"col": other})
            summed = summed + part_in[other, piece]
        yg[rep, piece] = summed
        line_step(yg, y_send, y_recv, piece, 0)

    others(0)
    for gap in range(2, n_rep - 1):
        line_step(cg, c_send, c_recv, 0, gap)
    for piece in range(pieces):
        if piece + 1 < pieces:
            others(piece + 1)
        own_part(piece)
        if piece >= 2:
            line_step(yg, y_send, y_recv, piece - 2, 1)
    if n_rep > 2:
        line_step(cg, c_send, c_recv, 0, n_rep - 1)
    turned = weight[...].T
    t_high, t_low = split(turned)
    t_both = jnp.concatenate([t_high, t_low], 0)
    own = weight[pl.ds(pl.multiple_of(rep * quarter, quarter), quarter), :]
    o_high, o_low = split(own)
    o_both = jnp.concatenate([o_high, o_low], 0)
    scale = (2.0 / 3.141592653589793) ** 0.5

    def bend(v):
        return jnp.tanh(scale * (v + 0.044715 * (v * v * v)))

    w_part = None
    width = n_rep * quarter
    steps = [(piece + 2 * gap, gap, piece) for gap in range(1, n_rep) for piece in range(pieces)]
    for _, gap, piece in sorted(steps):
        if gap > 1 or piece + 2 >= pieces:
            line_step(yg, y_send, y_recv, piece, gap)
        if gap < n_rep - 1:
            continue
        gathered = jnp.concatenate([yg[origin, piece] for origin in range(n_rep)], 0)
        v = dot_split(t_both, t_high, *split(gathered), NN)
        pre[:, spans[piece]] = v
        t = bend(v)
        slope = 0.5 * (1.0 + t) + 0.5 * v * (1.0 - t * t) * (scale * (1.0 + 0.134145 * (v * v)))
        grad_pre = cg[:, 0, :, spans[piece]].reshape(width, short) * slope
        g_high, g_low = split(grad_pre)
        hg[col, piece] = dot_split(o_both, o_high, g_high, g_low, NN)
        for k in range(1, n_col):
            other = lax.rem(col + k, n_col)
            start(
                hg.at[col, piece], hg.at[col, piece], h_send.at[k, piece], h_recv.at[col, piece],
                {"col": other},
            )
        y_high, y_low = split(yg[rep, piece])
        term = dot_split(jnp.concatenate([y_high, y_low], 0), y_high, g_high, g_low, NT)
        w_part = term if w_part is None else w_part + term

    w_own[...] = w_part.reshape(w_own.shape)
    for k in range(1, peers):
        other, device = peer(k)
        start(w_own.at[other], w_in.at[me], w_send.at[k], w_recv.at[me], device)
    mine = pre[pl.ds(pl.multiple_of(rep * quarter, quarter), quarter), :]
    output[...] = 0.5 * mine * (1.0 + bend(mine))

    def parts_of(source):
        high, low = split(jnp.concatenate([hg[source, piece] for piece in range(pieces)], 1))
        return jnp.concatenate([high, low], 0), high

    def back(k, dest, stacked, high):
        source = lax.rem(col + k, n_col)
        span = pl.ds(pl.multiple_of(dest * stretch, stretch), stretch)
        term = dot_split(stacked, high, a_high[source, :, span], a_low[source, :, span], NN)
        z_own[dest] = z_own[dest] + term if k else term

    order = [far(k) * 2 + (1 - core) for k in range(1, n_y)] + [sibling]
    order += [far(k) * 2 + core for k in range(1, n_y)] + [row]
    mine = parts_of(col)
    for dest in order:
        back(0, dest, *mine)
    for k in range(1, n_col):
        other = lax.rem(col + k, n_col)
        for piece in range(pieces):
            arrived(hg.at[other, piece], h_recv.at[other, piece], {"col": other})
        theirs = parts_of(other)
        for place, dest in enumerate(order):
            back(k, dest, *theirs)
            if k == n_col - 1:
                ahead = place % n_y + 1
                spot = far(ahead)
                if place < n_y:
                    start(
                        z_own.at[dest], z_sib.at[spot], s_send.at[place], s_recv.at[spot],
                        {"row": sibling},
                    )
                elif place < n_row - 1:
                    arrived(z_sib.at[spot], s_recv.at[spot], {"row": sibling})
                    z_own[dest] = z_own[dest] + z_sib[spot]
                    start(
                        z_own.at[dest], z_far.at[y], f_send.at[ahead], f_recv.at[y], {"row": dest}
                    )

    w_sum = w_own[me]
    for k in range(1, peers):
        other, device = peer(k)
        arrived(w_in.at[other], w_recv.at[other], device)
        w_sum = w_sum + w_in[other]
    w_all[me] = w_sum * float(stretch * peers) ** (-0.5)
    for k in range(1, peers):
        other, device = peer(k)
        start(w_all.at[me], w_all.at[me], v_send.at[k], v_recv.at[me], device)

    arrived(z_sib.at[y], s_recv.at[y], {"row": sibling})
    total = z_own[row] + z_sib[y]
    for k in range(1, n_y):
        arrived(z_far.at[far(k)], f_recv.at[far(k)], {"row": far(k) * 2 + core})
        total = total + z_far[far(k)]
    input_grad[...] = total
    for k in range(1, peers):
        other, device = peer(k)
        arrived(w_all.at[other], v_recv.at[other], device)
    weight_grad[...] = w_all[...].reshape(weight_grad.shape)

    for copy in sent:
        copy.wait_send()
    for gap in range(n_rep - 1):
        for side in (1, -1):
            line_send(cg, c_send, c_recv, 0, gap, side, False)
            for piece in range(pieces):
                line_send(yg, y_send, y_recv, piece, gap, side, False)


def leave_kernel(*refs):
    count = len(refs) // 2
    for k in range(count):
        refs[count + k][...] = refs[k][...]


def leave(results):
    vmem = pl.BlockSpec(memory_space=pltpu.VMEM)
    return pl.pallas_call(
        leave_kernel,
        out_shape=tuple(jax.ShapeDtypeStruct(r.shape, r.dtype) for r in results),
        in_specs=[vmem] * len(results),
        out_specs=(vmem,) * len(results),
    )(*results)


def fused(
    n_row, n_col, n_rep, features, weight, cotangent, tile_values, tile_row, tile_col, tile_kind,
    tile_count,
):
    quarter, stretch = features.shape
    width = weight.shape[0]
    peers = n_row * n_col
    slots, edge, _ = tile_values.shape
    row_tiles, col_tiles = n_col * stretch // edge, n_row * stretch // edge
    parts = 8 if slots % 8 == 0 else 1
    dense = (n_col, stretch, n_row * stretch)
    pieces = stretch // edge
    cut = (pieces, quarter, stretch // pieces)
    block = (quarter, stretch)
    vmem = pl.BlockSpec(memory_space=pltpu.VMEM)
    smem = pl.BlockSpec(memory_space=pltpu.SMEM)
    dma = pltpu.SemaphoreType.DMA
    piece = (peers, quarter // peers, width)
    n_y = n_row // 2
    results = pl.pallas_call(
        functools.partial(layer_kernel, n_row, n_col, n_rep),
        out_shape=(
            jax.ShapeDtypeStruct(block, F32),
            jax.ShapeDtypeStruct(block, F32),
            jax.ShapeDtypeStruct((quarter, width), F32),
        ),
        in_specs=[smem] * 2 + [vmem] * 2 + [pl.BlockSpec(memory_space=pltpu.HBM)] * 4,
        out_specs=(vmem,) * 3,
        scratch_shapes=[
            pltpu.VMEM((1, slots), jnp.int32),
            pltpu.VMEM((1, row_tiles * col_tiles), jnp.int32),
            pltpu.SMEM((1, slots), jnp.int32),
            pltpu.SMEM((1, row_tiles * col_tiles), jnp.int32),
            pltpu.VMEM(tile_values.shape, F32),
            pltpu.VMEM((slots + 1, edge, edge), F32),
            pltpu.VMEM(weight.shape, F32),
            pltpu.VMEM(dense, BF16),
            pltpu.VMEM(dense, BF16),
            pltpu.VMEM((n_row * stretch, 2 * quarter), BF16),
            pltpu.VMEM((n_row, *block), F32),
            pltpu.VMEM((n_rep, 1, *block), F32),
            pltpu.VMEM((n_rep, *cut), F32),
            pltpu.VMEM((n_col, *cut), F32),
            pltpu.VMEM((n_col, *cut), F32),
            pltpu.VMEM((n_rep * quarter, stretch), F32),
            pltpu.VMEM((n_col, *cut), F32),
            pltpu.VMEM((n_row, *block), F32),
            pltpu.VMEM((n_y, *block), F32),
            pltpu.VMEM((n_y, *block), F32),
            pltpu.VMEM(piece, F32),
            pltpu.VMEM(piece, F32),
            pltpu.VMEM(piece, F32),
            dma((2,)), dma((3,)), dma((parts,)),
            dma((n_row,)), dma((n_row,)),
            dma((2, n_rep, 1)), dma((n_rep, 1)),
            dma((2, n_rep, pieces)), dma((n_rep, pieces)),
            dma((n_col, pieces)), dma((n_col, pieces)),
            dma((n_col, pieces)), dma((n_col, pieces)),
            dma((n_y,)), dma((n_y,)),
            dma((n_y,)), dma((n_y,)),
            dma((peers,)), dma((peers,)),
            dma((peers,)), dma((peers,)),
        ],
        compiler_params=pltpu.CompilerParams(
            collective_id=0, has_side_effects=True, vmem_limit_bytes=56 * 2**20
        ),
    )(tile_kind, tile_count, tile_row, tile_col, features, weight, cotangent, tile_values)
    return leave(results)


def tile_terms(source, values, from_tile, to_tile, tile_kinds, live_weight, dest_tiles, transposed):
    feat_width = source.shape[0]
    tile_edge = values.shape[1]
    tiled = source.reshape(feat_width, source.shape[1] // tile_edge, tile_edge)
    picked = jnp.take(tiled, from_tile, axis=1)
    chosen = jnp.take(values, tile_kinds, axis=0)
    if transposed:
        products = jnp.einsum("fga,gab->fgb", picked, chosen, precision=lax.Precision.HIGHEST)
    else:
        products = jnp.einsum("fgb,gab->fga", picked, chosen, precision=lax.Precision.HIGHEST)
    onehot = (to_tile[:, None] == jnp.arange(dest_tiles, dtype=jnp.int32)[None, :]).astype(
        jnp.float32
    )
    onehot = onehot * live_weight[:, None]
    spread = jnp.einsum("fgt,gd->fdt", products, onehot, precision=lax.Precision.HIGHEST)
    return spread.reshape(feat_width, dest_tiles * tile_edge)


def aggregate(source, values, from_tile, to_tile, tile_kinds, live_count, dest_tiles, transposed):
    slot_total = tile_kinds.shape[0]
    live_weight = (jnp.arange(slot_total, dtype=jnp.int32) < live_count).astype(jnp.float32)
    return tile_terms(
        source, values, from_tile, to_tile, tile_kinds, live_weight, dest_tiles, transposed
    )


def local(features, weight, cotangent, tile_values, tile_row, tile_col, tile_kind, tile_count):
    n_rowdev = lax.axis_size("row")
    n_coldev = lax.axis_size("col")
    n_repdev = lax.axis_size("rep")
    quarter, stretch_len = features.shape
    nodes = n_rowdev * n_coldev
    if (
        n_rowdev * n_coldev * stretch_len * stretch_len * 4 <= DENSE_BYTES
        and n_rowdev % 2 == 0
        and n_coldev > 1
        and n_repdev > 1
        and quarter % (8 * nodes) == 0
        and tile_values.size * 4 <= DENSE_BYTES
    ):
        return fused(
            n_rowdev, n_coldev, n_repdev, features, weight, cotangent, tile_values,
            tile_row, tile_col, tile_kind, tile_count,
        )
    own_rows = lax.dynamic_slice_in_dim(weight, lax.axis_index("rep") * quarter, quarter, 0)
    tile_edge = tile_values.shape[1]
    live_count = tile_count[0]
    row_tiles = n_coldev * stretch_len // tile_edge
    col_tiles = n_rowdev * stretch_len // tile_edge
    mixed = lax.psum_scatter(
        lax.dot_general(
            own_rows,
            features,
            (((0,), (0,)), ((), ())),
            precision=lax.Precision.HIGHEST,
            preferred_element_type=jnp.float32,
        ),
        "rep",
        scatter_dimension=0,
        tiled=True,
    )
    column_block = lax.all_gather(mixed, "row", axis=1, tiled=True)
    partial_value = aggregate(
        column_block, tile_values, tile_col, tile_row, tile_kind, live_count, row_tiles, False
    )
    summed = lax.psum_scatter(partial_value, "col", scatter_dimension=1, tiled=True)
    output, pullback = jax.vjp(lambda v: jax.nn.gelu(v, approximate=True), summed)
    (grad_pre,) = pullback(cotangent)
    row_block = lax.all_gather(grad_pre, "col", axis=1, tiled=True)
    partial_back = aggregate(
        row_block, tile_values, tile_row, tile_col, tile_kind, live_count, col_tiles, True
    )
    grad_mixed = lax.psum_scatter(partial_back, "row", scatter_dimension=1, tiled=True)
    whole = lax.all_gather(grad_mixed, "rep", axis=0, tiled=True)
    input_grad = jnp.dot(
        own_rows, whole, preferred_element_type=jnp.float32, precision=lax.Precision.HIGHEST
    )
    weight_part = lax.dot_general(
        features,
        whole,
        (((1,), (1,)), ((), ())),
        precision=lax.Precision.HIGHEST,
        preferred_element_type=jnp.float32,
    )
    node_total = stretch_len * n_rowdev * n_coldev
    weight_grad = lax.psum(weight_part * float(node_total) ** (-0.5), ("row", "col"))
    return (output, input_grad, weight_grad)


def solution(mesh):
    return jax.shard_map(
        local,
        mesh=mesh,
        in_specs=(
            P("rep", ("col", "row")),
            P(),
            P("rep", ("row", "col")),
            P(("row", "col"), None, None),
            P(("row", "col")),
            P(("row", "col")),
            P(("row", "col")),
            P(("row", "col")),
        ),
        out_specs=(P("rep", ("row", "col")), P("rep", ("col", "row")), P("rep", None)),
        check_vma=False,
    )
```

profile of v0, /device:TPU:0, one launch (start us, length us, event | category | flops | bytes accessed | tf_op | source)
XLA Modules:
  0.0 48.0 jit_solution(27628243520182118)
XLA Ops:
  1.3 45.0 %shard_map.103 = (f32[64,512]{1,0:T(8,128)}, f32[64,512]{1,0:T(8,128)}, f32[64,256]{1,0:T(8,128)}) custom-call(s32[160]{0:T(256)} %kind.1, s32[1]{0:T(128)S(6)} %copy.11.count, s32[160]{0:T(256)} %tile_row.1, s32[160]{0:T(256)} %tile_col.1, f32[64,512]{1,0:T(8,128)} %features_in.1, f32[256,256]{1,0:T(8,128)} %weight_in.1, f32[64,512]{1,0:T(8,128)} %cotangent_in.1, ...), custom_call_target="tpu_custom_call" | custom-call | tf_op jit(solution)/shard_map/pallas_call | solution.py:399
  46.3 1.7 %shard_map.104 = (f32[64,512]{1,0:T(8,128)}, f32[64,512]{1,0:T(8,128)}, f32[64,256]{1,0:T(8,128)}) custom-call(f32[64,512]{1,0:T(8,128)} %get-tuple-element.6.refs_0_, f32[64,512]{1,0:T(8,128)} %get-tuple-element.7.refs_1_, f32[64,256]{1,0:T(8,128)} %get-tuple-element.8.refs_2_), custom_call_target="tpu_custom_call" | custom-call | tf_op jit(solution)/shard_map/pallas_call | solution.py:372
where the time goes:
time: 48.2 us; the launch traced here: 48 us
  Pallas kernels  46.7 us (97%)
  between operations  1.29 us (3%)
    pallas_call x1, Pallas kernels, fused(): pl.pallas_call(functools.partial(layer_kernel, n_row, n_col, n_rep), out_...  45 us
    pallas_call x1, Pallas kernels, leave(): pl.pallas_call(leave_kernel, out_shape=tuple((jax.ShapeDtypeStruct(r.shap...  1.7 us

commit v1 on v0

--- a/solution.py
+++ b/solution.py
@@ -171,7 +171,7 @@
         copy.wait()
     chain[slots] = jnp.zeros((edge, edge), F32)
 
-    @pl.loop(0, slots, unroll=4 if slots % 4 == 0 else 1)
+    @pl.loop(0, slots, unroll=8 if slots % 8 == 0 else 1)
     def _(slot):
         chain[slot] = held[kind[slot]] + chain[before[0, slot]]
 
@@ -209,8 +209,11 @@
 
     def aggregate_piece(dest, piece):
         nodes = xs[...]
-        term = jnp.dot(a_high[dest, spans[piece], :], nodes, preferred_element_type=F32)
-        term += jnp.dot(a_low[dest, spans[piece], :], nodes, preferred_element_type=F32)
+        rows = jnp.concatenate(
+            [a_high[dest, spans[piece], :], a_low[dest, spans[piece], :]], 0
+        )
+        term = jnp.dot(rows, nodes, preferred_element_type=F32)
+        term = term[:short] + term[short:]
         term = term.T
         return term[:quarter] + term[quarter:]
 

time: 48.2 us -> 48.2 us (level)
  no operation moved by 1% of the time
where the time goes in v1:
time: 48.2 us; the launch traced here: 48.1 us
  Pallas kernels  46.8 us (97%)
  between operations  1.29 us (3%)
    pallas_call x1, Pallas kernels, fused(): pl.pallas_call(functools.partial(layer_kernel, n_row, n_col, n_rep), out_...  45.1 us
    pallas_call x1, Pallas kernels, leave(): pl.pallas_call(leave_kernel, out_shape=tuple((jax.ShapeDtypeStruct(r.shap...  1.7 us

profile of v1, /device:TPU:0, one launch (start us, length us, event | category | flops | bytes accessed | tf_op | source)
XLA Modules:
  0.0 48.1 jit_solution(15208212576473991709)
XLA Ops:
  1.3 45.1 %shard_map.103 = (f32[64,512]{1,0:T(8,128)}, f32[64,512]{1,0:T(8,128)}, f32[64,256]{1,0:T(8,128)}) custom-call(s32[160]{0:T(256)} %kind.1, s32[1]{0:T(128)S(6)} %copy.11.count, s32[160]{0:T(256)} %tile_row.1, s32[160]{0:T(256)} %tile_col.1, f32[64,512]{1,0:T(8,128)} %features_in.1, f32[256,256]{1,0:T(8,128)} %weight_in.1, f32[64,512]{1,0:T(8,128)} %cotangent_in.1, ...), custom_call_target="tpu_custom_call" | custom-call | tf_op jit(solution)/shard_map/pallas_call | solution.py:402
  46.4 1.7 %shard_map.104 = (f32[64,512]{1,0:T(8,128)}, f32[64,512]{1,0:T(8,128)}, f32[64,256]{1,0:T(8,128)}) custom-call(f32[64,512]{1,0:T(8,128)} %get-tuple-element.6.refs_0_, f32[64,512]{1,0:T(8,128)} %get-tuple-element.7.refs_1_, f32[64,256]{1,0:T(8,128)} %get-tuple-element.8.refs_2_), custom_call_target="tpu_custom_call" | custom-call | tf_op jit(solution)/shard_map/pallas_call | solution.py:375
